TPU v7x, 32 devices: a whole 2x2x4 slice. The times are simulated.
32 devices in a mesh: groups: 2 (over y), space: 16 (over z, x, core).
Axes of the slice: x: 2, y: 2, z: 4, core: 2. Of those that a mesh axis runs over, the one named last changes fastest.
Arguments:
- actions: float32 [32, 8, 16, 2, 128], P(('groups', 'space')), parts along dimension 0, may hold values from -160 to 160
Outputs:
- q_fields: float32 [32, 8, 16, 2, 128], P(('groups', 'space')), parts along dimension 0
- r_factor: float32 [128, 64], P('groups'), parts along dimension 0
- first_factor: float32 [128, 64], P('groups'), parts along dimension 0
There are 2 independent parts, one for each index of `groups`. A program takes and returns all parts, laid end to end along the dimension named above; each array names one. Nothing has to cross between parts.
All inputs are finite; a program needn't handle non-finite values.
Results may differ from a plain program's by a relative error of at most 0.0003.
Values sent between devices are 32-bit elements; how exact they have to be, the bound alone decides.
A program may use at most 64 MiB of HBM per device.

v0:
```python
import math

import jax
import jax.numpy as jnp
from jax import lax
from jax.sharding import PartitionSpec as P

K = 64
SWEEPS = 3


damping = 1.0 / 7.0
highest = lax.Precision.HIGHEST


def shifted(shard, axis, by):
    peers = lax.axis_size(axis)
    pairs = [(i, i + by) for i in range(peers) if 0 <= i + by < peers]
    return lax.ppermute(shard, axis, pairs)


def neighbours(padded):
    total = padded[..., 2:, 1:-1, 1:-1] + padded[..., :-2, 1:-1, 1:-1]
    total = total + padded[..., 1:-1, 2:, 1:-1] + padded[..., 1:-1, :-2, 1:-1]
    total = total + padded[..., 1:-1, 1:-1, 2:] + padded[..., 1:-1, 1:-1, :-2]
    return total


def factor(gram):
    factor_low = jnp.linalg.cholesky(gram)
    identity = jnp.eye(gram.shape[0], dtype=gram.dtype)
    inverse = lax.linalg.triangular_solve(factor_low, identity, left_side=True, lower=True)
    return (factor_low, inverse)


def to_space(stacked):
    arrived = lax.all_to_all(stacked[None], "space", split_axis=2, concat_axis=0, tiled=True)
    senders, probe_group, width_x, rows_y, depth_z = arrived.shape
    group_count = K // probe_group
    slab_count = senders // group_count
    arranged = arrived.reshape(slab_count, group_count, probe_group, width_x, rows_y, depth_z)
    arranged = arranged.transpose(1, 2, 3, 0, 4, 5)
    return arranged.reshape(K, width_x, slab_count * rows_y, depth_z)


def to_probes(basis, probe_group):
    width_x, rows_all, depth_z = basis.shape[1:]
    group_count = K // probe_group
    senders = lax.axis_size("space")
    slab_count = senders // group_count
    rows_y = rows_all // slab_count
    arranged = basis.reshape(group_count, probe_group, width_x, slab_count, rows_y, depth_z)
    arranged = arranged.transpose(3, 0, 1, 2, 4, 5).reshape(
        senders, probe_group, width_x, rows_y, depth_z
    )
    return lax.all_to_all(arranged, "space", split_axis=0, concat_axis=2, tiled=True)


def smooth_probes(fields):
    probe_group = fields.shape[0]
    group_count = K // probe_group
    smoothed = fields * damping
    for sweep_index in range(SWEEPS):
        lower_rim = shifted(smoothed[:, :, -1:], "space", group_count)
        upper_rim = shifted(smoothed[:, :, :1], "space", -group_count)
        extended = jnp.concatenate([lower_rim, smoothed, upper_rim], axis=2)
        padded = jnp.pad(extended, ((0, 0), (1, 1), (0, 0), (1, 1)))
        smoothed = (fields + neighbours(padded)) * damping
    return smoothed


def shards(actions):
    fields = actions[0]
    spread = to_space(smooth_probes(fields))
    matrix = spread.reshape(K, -1)
    partial_one = jnp.dot(matrix, matrix.T, precision=highest, preferred_element_type=jnp.float32)
    gram_one = lax.psum(partial_one, "space")
    low_one, inverse_one = factor(gram_one)
    basis_one = jnp.dot(inverse_one, matrix, precision=highest, preferred_element_type=jnp.float32)
    partial_two = jnp.dot(
        basis_one, basis_one.T, precision=highest, preferred_element_type=jnp.float32
    )
    gram_two = lax.psum(partial_two, "space")
    low_two, inverse_two = factor(gram_two)
    basis = jnp.dot(inverse_two, basis_one, precision=highest, preferred_element_type=jnp.float32)
    scale = math.sqrt(lax.axis_size("space") * matrix.shape[1])
    q_fields = to_probes((basis * scale).reshape(spread.shape), fields.shape[0])
    r_factor = (
        jnp.dot(low_one, low_two, precision=highest, preferred_element_type=jnp.float32).T / scale
    )
    first_factor = low_one.T / scale
    return (q_fields, r_factor, first_factor)


def solution(mesh):
    in_specs = (P(("groups", "space"), None, None, None, None),)
    out_specs = (
        P(("groups", "space"), None, None, None, None),
        P("groups", None),
        P("groups", None),
    )
    return jax.shard_map(shards, mesh=mesh, in_specs=in_specs, out_specs=out_specs, check_vma=False)
```

profile of v0, /device:TPU:0, one launch (start us, length us, event | category | flops | bytes accessed | tf_op | source)
XLA Modules:
  0.0 199.6 jit_solution(11168783792871111746)
XLA Ops:
  0.6 1.0 bitcast_multiply_fusion
  1.6 5.9 %collective-permute-start = (f32[8,16,1,128]{3,0,2,1:T(8,128)S(1)}, f32[8,16,1,128]{3,0,2,1:T(8,128)S(1)}, u32[]{:S(2)}, u32[]{:S(2)}) collective-permute-start(f32[8,16,1,128]{3,0,2,1:T(8,128)S(1)} %get-tuple-element.21), channel_id=1, source_target_pairs={{0,8},{1,9},{2,10},{3,11},{4,12},{5,13},{6,14},{7,15},{16,24},{17,... | collective-permute-start | bytes 196616 | tf_op jit(solution)/shard_map/ppermute | solution.py:19
  7.6 1.4 collective-permute-start.1
  9.5 5.6 %collective-permute-done.1 = f32[8,16,1,128]{3,0,2,1:T(8,128)S(1)} collective-permute-done((f32[8,16,1,128]{3,0,2,1:T(8,128)S(1)}, f32[8,16,1,128]{3,0,2,1:T(8,128)S(1)}, u32[]{:S(2)}, u32[]{:S(2)}) %collective-permute-start.1) | collective-permute-done | bytes 65568 | tf_op jit(solution)/shard_map/ppermute | solution.py:19
  15.5 1.5 collective-permute-start.2
  17.0 1.3 collective-permute-start.3
  18.9 5.2 %collective-permute-done.3 = f32[8,16,1,128]{3,0,2,1:T(8,128)S(1)} collective-permute-done((f32[8,16,1,128]{3,0,2,1:T(8,128)S(1)}, f32[8,16,1,128]{3,0,2,1:T(8,128)S(1)}, u32[]{:S(2)}, u32[]{:S(2)}) %collective-permute-start.3) | collective-permute-done | bytes 65568 | tf_op jit(solution)/shard_map/ppermute | solution.py:19
  24.4 1.6 collective-permute-start.4
  26.0 1.3 collective-permute-start.5
  27.9 5.2 %collective-permute-done.5 = f32[8,16,1,128]{3,0,2,1:T(8,128)S(1)} collective-permute-done((f32[8,16,1,128]{3,0,2,1:T(8,128)S(1)}, f32[8,16,1,128]{3,0,2,1:T(8,128)S(1)}, u32[]{:S(2)}, u32[]{:S(2)}) %collective-permute-start.5) | collective-permute-done | bytes 65568 | tf_op jit(solution)/shard_map/ppermute | solution.py:19
  33.5 11.4 %all_to_all.33 = f32[1,8,16,2,128]{4,1,3,0,2:T(8,128)S(1)} all-to-all(f32[1,8,16,2,128]{4,1,3,0,2:T(8,128)S(1)} %fusion.5), channel_id=1, replica_groups=mesh['groups'=2,'space'=16] {'space'}, dimensions={2} | all-to-all | bytes 262144 | tf_op jit(solution)/shard_map/all_to_all | solution.py:37
  45.2 58.2 %psum.14 = f32[64,64]{0,1:T(8,128)S(1)} all-reduce(f32[64,64]{0,1:T(8,128)S(1)} %fusion.41), channel_id=1, replica_groups=mesh['groups'=2,'space'=16] {'space'}, use_global_device_ids=true, to_apply=%region_0.1 | all-reduce | flops 4096 | bytes 32768 | tf_op jit(solution)/shard_map/psum | solution.py:77
  103.5 5.8 %cholesky.44 = f32[64,64]{1,0:T(8,128)S(1)} custom-call(f32[64,64]{1,0:T(8,128)S(1)} %fusion.23), custom_call_target="Cholesky" | custom-call | tf_op jit(solution)/shard_map/jit(cholesky)/cholesky | solution.py:30
  109.3 0.7 compare_reduce_fusion.1
  110.8 4.9 %custom-call.6 = f32[1,64,64]{1,2,0:T(8,128)S(1)} custom-call(f32[1,64,64]{2,1,0:T(8,128)S(1)} %get-tuple-element.24), custom_call_target="InvertDiagBlocksLowerTriangular" | custom-call | tf_op jit(solution)/shard_map/triangular_solve/custom-call.0 | solution.py:32
  116.5 57.6 %psum.15 = f32[64,64]{0,1:T(8,128)S(1)} all-reduce(f32[64,64]{0,1:T(8,128)S(1)} %fusion.43), channel_id=1, replica_groups=mesh['groups'=2,'space'=16] {'space'}, use_global_device_ids=true, to_apply=%region_3.6 | all-reduce | flops 4096 | bytes 32768 | tf_op jit(solution)/shard_map/psum | solution.py:83
  174.2 5.8 %cholesky.55 = f32[64,64]{1,0:T(8,128)S(1)} custom-call(f32[64,64]{1,0:T(8,128)S(1)} %fusion.21), custom_call_target="Cholesky" | custom-call | tf_op jit(solution)/shard_map/jit(cholesky)/cholesky | solution.py:30
  181.3 4.9 %custom-call.7 = f32[1,64,64]{1,2,0:T(8,128)S(1)} custom-call(f32[1,64,64]{2,1,0:T(8,128)S(1)} %select_bitcast_fusion), custom_call_target="InvertDiagBlocksLowerTriangular" | custom-call | tf_op jit(solution)/shard_map/triangular_solve/custom-call.0 | solution.py:32
  186.7 0.7 copy.30
  187.4 3.5 %all-to-all-start.1 = ((f32[16,8,1,2,128]{4,3,1,2,0:T(2,128)}), f32[16,8,1,2,128]{4,3,1,2,0:T(2,128)S(1)}, u32[]{:S(2)}, u32[]{:S(2)}) async-start(f32[16,8,1,2,128]{4,3,1,2,0:T(2,128)} %bitcast.15), calls=%async_computation.1 | async-start | bytes 262144 | tf_op jit(solution)/shard_map/all_to_all | solution.py:56
  190.9 0.7 copy.32
  191.6 2.1 %convolution_multiply_fusion.1 = f32[64,64]{1,0:T(8,128)} fusion(f32[64,64]{1,0:T(8,128)S(1)} %cholesky.55, f32[64,64]{1,0:T(8,128)S(1)} %cholesky.44, pred[]{:T(512)} %compare_reduce_fusion, pred[]{:T(512)} %compare_reduce_fusion.1), kind=kOutput, calls=%fused_computation.1 | convolution fusion | flops 3174400 | bytes 49154 | tf_op jit(solution)/shard_map/dot_general | solution.py:89
  193.7 5.1 %all-to-all-done.1 = f32[16,8,1,2,128]{4,3,1,2,0:T(2,128)S(1)} async-done(((f32[16,8,1,2,128]{4,3,1,2,0:T(2,128)}), f32[16,8,1,2,128]{4,3,1,2,0:T(2,128)S(1)}, u32[]{:S(2)}, u32[]{:S(2)}) %all-to-all-start.1) | async-done | bytes 131104 | tf_op jit(solution)/shard_map/all_to_all | solution.py:56
  198.8 0.7 copy.31
  (30 shorter events, 6.4 us)
Async XLA Ops:
  1.6 7.8 %collective-permute-start = (f32[8,16,1,128]{3,0,2,1:T(8,128)S(1)}, f32[8,16,1,128]{3,0,2,1:T(8,128)S(1)}, u32[]{:S(2)}, u32[]{:S(2)}) collective-permute-start(f32[8,16,1,128]{3,0,2,1:T(8,128)S(1)} %get-tuple-element.21), channel_id=1, source_target_pairs={{0,8},{1,9},{2,10},{3,11},{4,12},{5,13},{6,14},{7,15},{16,24},{17,... | collective-permute-start | bytes 196616 | tf_op jit(solution)/shard_map/ppermute | solution.py:19
  7.6 7.7 %copy-start = (f32[1,8,16,2,128]{4,3,2,1,0:T(2,128)S(1)}, f32[1,8,16,2,128]{4,3,2,1,0:T(2,128)}, u32[]{:S(2)}) copy-start(f32[1,8,16,2,128]{4,3,2,1,0:T(2,128)} %param.4) | copy-start | bytes 393220
  7.6 7.5 %collective-permute-start.1 = (f32[8,16,1,128]{3,0,2,1:T(8,128)S(1)}, f32[8,16,1,128]{3,0,2,1:T(8,128)S(1)}, u32[]{:S(2)}, u32[]{:S(2)}) collective-permute-start(f32[8,16,1,128]{3,0,2,1:T(8,128)S(1)} %get-tuple-element.22), channel_id=1, source_target_pairs={{8,0},{9,1},{10,2},{11,3},{12,4},{13,5},{14,6},{15,7},{24,16},{25,... | collective-permute-start | bytes 196616 | tf_op jit(solution)/shard_map/ppermute | solution.py:19
  15.5 3.3 %collective-permute-start.2 = (f32[8,16,1,128]{3,0,2,1:T(8,128)S(1)}, f32[8,16,1,128]{3,0,2,1:T(8,128)S(1)}, u32[]{:S(2)}, u32[]{:S(2)}) collective-permute-start(f32[8,16,1,128]{3,0,2,1:T(8,128)S(1)} %get-tuple-element.19), channel_id=1, source_target_pairs={{0,8},{1,9},{2,10},{3,11},{4,12},{5,13},{6,14},{7,15},{16,24},{17,... | collective-permute-start | bytes 196616 | tf_op jit(solution)/shard_map/ppermute | solution.py:19
  17.0 7.1 %collective-permute-start.3 = (f32[8,16,1,128]{3,0,2,1:T(8,128)S(1)}, f32[8,16,1,128]{3,0,2,1:T(8,128)S(1)}, u32[]{:S(2)}, u32[]{:S(2)}) collective-permute-start(f32[8,16,1,128]{3,0,2,1:T(8,128)S(1)} %get-tuple-element.20), channel_id=1, source_target_pairs={{8,0},{9,1},{10,2},{11,3},{12,4},{13,5},{14,6},{15,7},{24,16},{25,... | collective-permute-start | bytes 196616 | tf_op jit(solution)/shard_map/ppermute | solution.py:19
  24.4 3.5 %collective-permute-start.4 = (f32[8,16,1,128]{3,0,2,1:T(8,128)S(1)}, f32[8,16,1,128]{3,0,2,1:T(8,128)S(1)}, u32[]{:S(2)}, u32[]{:S(2)}) collective-permute-start(f32[8,16,1,128]{3,0,2,1:T(8,128)S(1)} %get-tuple-element.17), channel_id=1, source_target_pairs={{0,8},{1,9},{2,10},{3,11},{4,12},{5,13},{6,14},{7,15},{16,24},{17,... | collective-permute-start | bytes 196616 | tf_op jit(solution)/shard_map/ppermute | solution.py:19
  26.0 7.1 %collective-permute-start.5 = (f32[8,16,1,128]{3,0,2,1:T(8,128)S(1)}, f32[8,16,1,128]{3,0,2,1:T(8,128)S(1)}, u32[]{:S(2)}, u32[]{:S(2)}) collective-permute-start(f32[8,16,1,128]{3,0,2,1:T(8,128)S(1)} %get-tuple-element.18), channel_id=1, source_target_pairs={{8,0},{9,1},{10,2},{11,3},{12,4},{13,5},{14,6},{15,7},{24,16},{25,... | collective-permute-start | bytes 196616 | tf_op jit(solution)/shard_map/ppermute | solution.py:19
  187.4 11.4 %all-to-all-start.1 = ((f32[16,8,1,2,128]{4,3,1,2,0:T(2,128)}), f32[16,8,1,2,128]{4,3,1,2,0:T(2,128)S(1)}, u32[]{:S(2)}, u32[]{:S(2)}) async-start(f32[16,8,1,2,128]{4,3,1,2,0:T(2,128)} %bitcast.15), calls=%async_computation.1 | async-start | bytes 262144 | tf_op jit(solution)/shard_map/all_to_all | solution.py:56
where the time goes:
time: 200 us
  blocking collectives  127 us (64%)
  other arithmetic  26.3 us (13%)
  waiting for transfers between devices  22.7 us (11%)
  starting transfers between devices  16.5 us (8%)
  matrix products  3.64 us (2%)
  local copies, waits for them, and re-layouts  2.33 us (1%)
    psum x1, blocking collectives, shards(): gram_one = lax.psum(partial_one, 'space')  58.2 us
    psum x1, blocking collectives, shards(): gram_two = lax.psum(partial_two, 'space')  57.6 us
    ppermute x6, waiting for transfers between devices, shifted(): return lax.ppermute(shard, axis, pairs)  17.6 us
    another operation x6, other arithmetic, factor(): factor_low = jnp.linalg.cholesky(gram)  13.1 us
    ppermute x6, starting transfers between devices, shifted(): return lax.ppermute(shard, axis, pairs)  13 us
    all_to_all x1, blocking collectives, to_space(): lax.all_to_all(stacked[None], 'space', split_axis=2, concat_axis=0, tiled...  11.4 us
    another operation x3, other arithmetic, factor(): lax.linalg.triangular_solve(factor_low, identity, left_side=True, lower=T...  10.4 us
    all_to_all x1, waiting for transfers between devices, to_probes(): lax.all_to_all(arranged, 'space', split_axis=0, concat_axis=2, tiled=True)  5.1 us
  transfers between devices with their start and end apart: 7, of which 7 were waited for; matrix products, arithmetic and copies ran while one was open for 1% of the time, Pallas kernels for 0%

commit v1 on v0

v1 whole, which is shorter than its diff:
```python
import functools
import math

import jax
import jax.numpy as jnp
from jax import lax
from jax.experimental import pallas as pl
from jax.experimental.pallas import tpu as pltpu
from jax.sharding import PartitionSpec as P

K = 64
YS = 2
highest = lax.Precision.HIGHEST
MESH = pl.DeviceIdType.MESH


def slab_offsets(slabs):
    return sorted({d % slabs for d in (1, -1, 2, -2)} - {0})


def walks(p, q, rows):
    gap = jnp.abs(p - q)
    low, high = jnp.minimum(p, q), jnp.maximum(p, q)
    at_start = jnp.where(low == 0, 1, 0)
    at_end = jnp.where(high == rows - 1, 1, 0)
    one = jnp.where(gap == 1, 1, 0)
    two = jnp.where(gap == 2, 1, 0) + jnp.where(gap == 0, 2 - at_start - at_end, 0)
    three = jnp.where(gap == 3, 1, 0) + jnp.where(gap == 1, 3 - at_start - at_end, 0)
    return one.astype(jnp.float32), two.astype(jnp.float32), three.astype(jnp.float32)


def eliminate(gram):
    lane = lax.broadcasted_iota(jnp.int32, (K, 128), 1)
    row_id = lax.broadcasted_iota(jnp.int32, (K, 128), 0)
    full = jnp.where(lane < K, gram, jnp.where(lane - K == row_id, 1.0, 0.0))
    blocks = [full[8 * i : 8 * i + 8] for i in range(K // 8)]
    sub = lax.broadcasted_iota(jnp.int32, (8, 128), 0)
    count = len(blocks)
    shape = (8, 128)
    scaled = []
    for t in range(count):
        cols = [
            {i: jnp.broadcast_to(blocks[i][:, 8 * t + k : 8 * t + k + 1], shape) for i in range(t, count)}
            for k in range(8)
        ]
        pivots = jnp.ones(shape, jnp.float32)
        for r in range(8):
            pivot = jnp.broadcast_to(cols[r][t][r : r + 1], shape)
            pivots = jnp.where(sub == r, pivot, pivots)
            inverse = 1.0 / pivot
            factors = {i: cols[r][i] * inverse for i in range(t, count)}
            factors[t] = jnp.where(sub > r, factors[t], 0.0)
            for k in range(r + 1, 8):
                value = jnp.broadcast_to(cols[r][t][k : k + 1], shape)
                for i in range(t, count):
                    cols[k][i] = cols[k][i] - factors[i] * value
            row = jnp.broadcast_to(blocks[t][r : r + 1], shape)
            for i in range(t, count):
                blocks[i] = blocks[i] - factors[i] * row
        scaled.append(blocks[t] * lax.rsqrt(pivots))
    done = jnp.concatenate(scaled, axis=0)
    offset = jnp.where(lane < K, lane - row_id, row_id + K - lane)
    return jnp.where(offset >= 0, done, 0.0)


def kernel(
    slabs, groups, scale,
    fields, q_out, r_out, first_out,
    own_send, cross_send, own_recv, cross_recv, rs_send, rs_recv, ag_send, ag_recv, back_send,
    a_send, a_recv, c_send, c_recv, r_send, r_recv, g_send, g_recv, b_send, b_recv,
):
    devices = slabs * groups
    me = lax.axis_index("space")
    slab, group = me // groups, lax.rem(me, groups)
    offsets = slab_offsets(slabs)
    probe = K // groups
    cells = fields.shape[0] // probe
    width = cells // YS
    chunk = cells // groups

    barrier = pltpu.get_barrier_semaphore()
    for k in range(1, devices):
        pl.semaphore_signal(barrier, inc=1, device_id={"space": lax.rem(me + k, devices)}, device_id_type=MESH)

    field = jnp.stack([fields[pl.ds(c, probe, stride=cells), :] for c in range(cells)])
    field = field.reshape(width, YS, probe, 128)
    lane = lax.broadcasted_iota(jnp.int32, (probe, 128), 1)
    not_first, not_last = lane > 0, lane < 127

    def plane(u):
        flat = u.reshape(cells * probe, 128)
        low = pltpu.roll(flat, 1, 1).reshape(u.shape)
        high = pltpu.roll(flat, 127, 1).reshape(u.shape)
        total = jnp.where(not_first, low, 0.0) + jnp.where(not_last, high, 0.0)
        edge = jnp.zeros((1,) + u.shape[1:], u.dtype)
        return total + jnp.concatenate([u[1:], edge], 0) + jnp.concatenate([edge, u[:-1]], 0)

    d = 1.0 / 7.0
    one = plane(field)
    two = plane(one)
    three = plane(two)
    q0 = field * d + one * d**2 + two * d**3 + three * d**4
    q1 = field * d**2 + one * (2 * d**3) + two * (3 * d**4)
    q2 = field * d**3 + one * (3 * d**4)
    q3 = field * d**4

    def spread(other, own):
        rows = []
        for b in range(YS):
            a = 1 - b
            _, w2, _ = walks(YS * slab + b, YS * other + b, YS * slabs)
            w1, _, w3 = walks(YS * slab + a, YS * other + b, YS * slabs)
            value = w2 * q2[:, b] + w1 * q1[:, a] + w3 * q3[:, a]
            rows.append(q0[:, b] + value if own else value)
        return jnp.stack(rows, axis=1).reshape(groups, chunk, probe, 128)

    for n, offset in enumerate(offsets):
        cross_send[n] = spread(lax.rem(slab + offset, slabs), False)

    pl.semaphore_wait(barrier, devices - 1)

    started = []

    def send(src, dst, send_sem, recv_sem, peer):
        copy = pltpu.make_async_remote_copy(
            src_ref=src, dst_ref=dst, send_sem=send_sem, recv_sem=recv_sem,
            device_id={"space": peer}, device_id_type=MESH,
        )
        copy.start()
        started.append(copy)

    def arrive(dst, sem):
        pltpu.make_async_copy(dst, dst, sem).wait()

    for n, offset in enumerate(offsets):
        there = lax.rem(slab + offset, slabs)
        for k in range(groups):
            g = lax.rem(group + k, groups)
            send(cross_send.at[n, g], cross_recv.at[n, group], c_send.at[n, g], c_recv.at[n, group], there * groups + g)
    own_send[...] = spread(slab, True)
    for k in range(1, groups):
        g = lax.rem(group + k, groups)
        send(own_send.at[g], own_recv.at[group], a_send.at[g], a_recv.at[group], slab * groups + g)
    own_recv[group] = own_send[group]
    for k in range(1, groups):
        g = lax.rem(group + k, groups)
        arrive(own_recv.at[g], a_recv.at[g])
    for n in range(len(offsets)):
        for g in range(groups):
            arrive(cross_recv.at[n, g], c_recv.at[n, g])
    total = own_recv[...]
    for n in range(len(offsets)):
        total = total + cross_recv[n]
    matrix = jnp.concatenate([total[:, c].reshape(K, 128) for c in range(chunk)], axis=1)

    def summed(rows, turn, precision):
        part = lax.dot_general(
            rows, rows, (((1,), (1,)), ((), ())), precision=precision, preferred_element_type=jnp.float32
        )
        part = jnp.concatenate([part, jnp.zeros((K, 128 - K), jnp.float32)], axis=1)
        rs_send[turn] = part.reshape(groups, probe, 128)
        for k in range(1, devices):
            peer = lax.rem(me + k, devices)
            send(rs_send.at[turn, lax.rem(peer, groups)], rs_recv.at[turn, me], r_send.at[turn, peer], r_recv.at[turn, me], peer)
        rs_recv[turn, me] = rs_send[turn, group]
        for k in range(1, devices):
            peer = lax.rem(me + k, devices)
            arrive(rs_recv.at[turn, peer], r_recv.at[turn, peer])
        ag_send[turn] = jnp.sum(rs_recv[turn], axis=0)
        for k in range(1, groups):
            g = lax.rem(group + k, groups)
            send(ag_send.at[turn], ag_recv.at[turn, group], g_send.at[turn, g], g_recv.at[turn, group], slab * groups + g)
        ag_recv[turn, group] = ag_send[turn]
        for k in range(1, groups):
            g = lax.rem(group + k, groups)
            arrive(ag_recv.at[turn, g], g_recv.at[turn, g])
        return ag_recv[turn].reshape(K, 128)

    both_one = eliminate(summed(matrix, 0, highest))
    basis_one = jnp.dot(both_one[:, K:], matrix, precision=highest, preferred_element_type=jnp.float32)
    both_two = eliminate(summed(basis_one, 1, highest))
    basis = jnp.dot(both_two[:, K:] * scale, basis_one, precision=highest, preferred_element_type=jnp.float32)
    for c in range(chunk):
        back_send[:, c] = basis[:, 128 * c : 128 * c + 128].reshape(groups, probe, 128)
    for k in range(1, groups):
        g = lax.rem(group + k, groups)
        send(back_send.at[g], q_out.at[group], b_send.at[g], b_recv.at[group], slab * groups + g)
    q_out[group] = back_send[group]
    first = both_one[:, :K]
    first_out[...] = first * (1.0 / scale)
    r_out[...] = jnp.dot(both_two[:, :K], first, precision=highest, preferred_element_type=jnp.float32) * (1.0 / scale)
    for k in range(1, groups):
        g = lax.rem(group + k, groups)
        arrive(q_out.at[g], b_recv.at[g])
    for copy in started:
        copy.wait_send()


def shards(actions):
    _, probe, width, rows_y, depth = actions.shape
    devices = lax.axis_size("space")
    groups = K // probe
    slabs = devices // groups
    cells = width * rows_y
    chunk = cells // groups
    others = len(slab_offsets(slabs))
    scale = math.sqrt(width * rows_y * slabs * depth)
    dma = pltpu.SemaphoreType.DMA
    block = (groups, chunk, probe, depth)
    f32 = jnp.float32
    vmem = pl.BlockSpec(memory_space=pltpu.VMEM)
    q, r, first = pl.pallas_call(
        functools.partial(kernel, slabs, groups, scale),
        out_shape=(
            jax.ShapeDtypeStruct(block, f32),
            jax.ShapeDtypeStruct((K, K), f32),
            jax.ShapeDtypeStruct((K, K), f32),
        ),
        in_specs=[vmem],
        out_specs=(vmem, vmem, vmem),
        scratch_shapes=[
            pltpu.VMEM(block, f32),
            pltpu.VMEM((others,) + block, f32),
            pltpu.VMEM(block, f32),
            pltpu.VMEM((others,) + block, f32),
            pltpu.VMEM((2, groups, probe, 128), f32),
            pltpu.VMEM((2, devices, probe, 128), f32),
            pltpu.VMEM((2, probe, 128), f32),
            pltpu.VMEM((2, groups, probe, 128), f32),
            pltpu.VMEM(block, f32),
            dma((groups,)), dma((groups,)),
            dma((others, groups)), dma((others, groups)),
            dma((2, devices)), dma((2, devices)),
            dma((2, groups)), dma((2, groups)),
            dma((groups,)), dma((groups,)),
        ],
        compiler_params=pltpu.CompilerParams(
            collective_id=0, has_side_effects=True, vmem_limit_bytes=48 * 1024 * 1024
        ),
    )(actions.reshape(probe * cells, depth))
    q_fields = q.reshape(cells, probe, depth).transpose(1, 0, 2)
    return (q_fields.reshape(1, probe, width, rows_y, depth), r, first)


def solution(mesh):
    in_specs = (P(("groups", "space"), None, None, None, None),)
    out_specs = (
        P(("groups", "space"), None, None, None, None),
        P("groups", None),
        P("groups", None),
    )
    return jax.shard_map(shards, mesh=mesh, in_specs=in_specs, out_specs=out_specs, check_vma=False)
```

time: 200 us -> 40.4 us (0.20)
  blocking collectives: 127 us -> 0 us
  Pallas kernels: 0 us -> 36.8 us
  other arithmetic: 26.3 us -> 0 us
  waiting for transfers between devices: 22.7 us -> 0 us
  starting transfers between devices: 16.5 us -> 0 us
  matrix products: 3.64 us -> 0 us
    psum x2 -> x0, blocking collectives: 116 us -> none  [the longest x1 58.2 us: shards(): gram_one = lax.psum(partial_one, 'space')]
    pallas_call x0 -> x1, Pallas kernels: none -> 36.8 us  [shards(): pl.pallas_call(functools.partial(kernel, slabs, groups, scale), out_shape...]
    another operation x9 -> x0, other arithmetic: 23.5 us -> none  [the longest x6 13.1 us: factor(): factor_low = jnp.linalg.cholesky(gram)]
    ppermute x6 -> x0, waiting for transfers between devices: 17.6 us -> none  [shifted(): return lax.ppermute(shard, axis, pairs)]
    ppermute x6 -> x0, starting transfers between devices: 13 us -> none  [shifted(): return lax.ppermute(shard, axis, pairs)]
    all_to_all x1 -> x0, blocking collectives: 11.4 us -> none  [to_space(): lax.all_to_all(stacked[None], 'space', split_axis=2, concat_axis=0, tiled...]
    all_to_all x1 -> x0, waiting for transfers between devices: 5.1 us -> none  [to_probes(): lax.all_to_all(arranged, 'space', split_axis=0, concat_axis=2, tiled=True)]
    all_to_all x1 -> x0, starting transfers between devices: 3.51 us -> none  [to_probes(): lax.all_to_all(arranged, 'space', split_axis=0, concat_axis=2, tiled=True)]
  transfers between devices with their start and end apart: 7 -> 0, of which waited for: 7 -> 0; matrix products, arithmetic and copies ran while one was open for 1% -> 0% of each run, Pallas kernels for 0% -> 0%
where the time goes in v1:
time: 40.4 us; the launch traced here: 40.2 us
  Pallas kernels  36.8 us (91%)
  local copies, waits for them, and re-layouts  2.81 us (7%)
  between operations  0.65 us (2%)
    pallas_call x1, Pallas kernels, shards(): pl.pallas_call(functools.partial(kernel, slabs, groups, scale), out_shape...  36.8 us
    unnamed x4, local copies, waits for them, and re-layouts  2.13 us

profile of v1, /device:TPU:0, one launch (start us, length us, event | category | flops | bytes accessed | tf_op | source)
XLA Modules:
  0.0 40.2 jit_solution(633105562041561961)
XLA Ops:
  0.6 0.0 copy-start
  0.6 0.9 %copy-done = f32[1,8,16,2,128]{4,3,2,1,0:T(2,128)S(1)} copy-done((f32[1,8,16,2,128]{4,3,2,1,0:T(2,128)S(1)}, f32[1,8,16,2,128]{4,3,2,1,0:T(2,128)}, u32[]{:S(2)}) %copy-start) | copy-done | bytes 131096
  1.5 36.8 %shard_map.38 = (f32[8,4,8,128]{3,2,1,0:T(8,128)S(1)}, f32[64,64]{1,0:T(8,128)S(1)}, f32[64,64]{1,0:T(8,128)S(1)}) custom-call(f32[256,128]{1,0:T(8,128)S(1)} %bitcast.5), custom_call_target="tpu_custom_call" | custom-call | tf_op jit(solution)/shard_map/pallas_call | solution.py:212
  38.3 0.7 %copy.4 = f32[8,32,128]{2,1,0:T(8,128)} copy(f32[8,32,128]{2,0,1:T(8,128)S(1)} %bitcast.6) | data formatting | bytes 262144 | tf_op jit(solution)/shard_map/transpose | solution.py:241
  39.0 0.6 %copy.7 = f32[64,64]{1,0:T(8,128)} copy(f32[64,64]{1,0:T(8,128)S(1)} %get-tuple-element.13) | data formatting | bytes 32768
  39.6 0.6 %copy.8 = f32[64,64]{1,0:T(8,128)} copy(f32[64,64]{1,0:T(8,128)S(1)} %get-tuple-element.14) | data formatting | bytes 32768
Async XLA Ops:
  0.6 0.9 %copy-start = (f32[1,8,16,2,128]{4,3,2,1,0:T(2,128)S(1)}, f32[1,8,16,2,128]{4,3,2,1,0:T(2,128)}, u32[]{:S(2)}) copy-start(f32[1,8,16,2,128]{4,3,2,1,0:T(2,128)} %param.1) | copy-start | bytes 393220

commit v2 on v1

--- a/solution.py
+++ b/solution.py
@@ -32,7 +32,8 @@
 def eliminate(gram):
     lane = lax.broadcasted_iota(jnp.int32, (K, 128), 1)
     row_id = lax.broadcasted_iota(jnp.int32, (K, 128), 0)
-    full = jnp.where(lane < K, gram, jnp.where(lane - K == row_id, 1.0, 0.0))
+    full = jnp.concatenate([gram, pltpu.roll(gram, K, 1)], axis=0)
+    full = jnp.where(lane < K, full, jnp.where(lane - K == row_id, 1.0, 0.0))
     blocks = [full[8 * i : 8 * i + 8] for i in range(K // 8)]
     sub = lax.broadcasted_iota(jnp.int32, (8, 128), 0)
     count = len(blocks)
@@ -65,9 +66,10 @@
 
 def kernel(
     slabs, groups, scale,
-    fields, q_out, r_out, first_out,
-    own_send, cross_send, own_recv, cross_recv, rs_send, rs_recv, ag_send, ag_recv, back_send,
-    a_send, a_recv, c_send, c_recv, r_send, r_recv, g_send, g_recv, b_send, b_recv,
+    source, q_out, factors_out,
+    fields,
+    own_send, cross_send, own_recv, cross_recv, part_send, part_recv, half_send, half_recv, back_send,
+    a_send, a_recv, c_send, c_recv, p_send, p_recv, h_send, h_recv, b_send, b_recv, in_sem,
 ):
     devices = slabs * groups
     me = lax.axis_index("space")
@@ -78,10 +80,14 @@
     width = cells // YS
     chunk = cells // groups
 
+    core = lax.rem(me, 2)
+    load = pltpu.make_async_copy(source, fields, in_sem)
+    load.start()
     barrier = pltpu.get_barrier_semaphore()
     for k in range(1, devices):
         pl.semaphore_signal(barrier, inc=1, device_id={"space": lax.rem(me + k, devices)}, device_id_type=MESH)
 
+    load.wait()
     field = jnp.stack([fields[pl.ds(c, probe, stride=cells), :] for c in range(cells)])
     field = field.reshape(width, YS, probe, 128)
     lane = lax.broadcasted_iota(jnp.int32, (probe, 128), 1)
@@ -157,24 +163,19 @@
         part = lax.dot_general(
             rows, rows, (((1,), (1,)), ((), ())), precision=precision, preferred_element_type=jnp.float32
         )
-        part = jnp.concatenate([part, jnp.zeros((K, 128 - K), jnp.float32)], axis=1)
-        rs_send[turn] = part.reshape(groups, probe, 128)
+        part = jnp.concatenate([part[: K // 2], part[K // 2 :]], axis=1)
+        part_send[turn] = part.reshape(2, K // 4, 128)
+        send(part_send.at[turn, 1 - core], part_recv.at[turn], p_send.at[turn], p_recv.at[turn], me + 1 - 2 * core)
+        arrive(part_recv.at[turn], p_recv.at[turn])
+        half_send[turn] = part_send[turn, core] + part_recv[turn]
+        for k in reversed(range(1, devices)):
+            peer = lax.rem(me + k, devices)
+            send(half_send.at[turn], half_recv.at[turn, me], h_send.at[turn, peer], h_recv.at[turn, me], peer)
+        half_recv[turn, me] = half_send[turn]
         for k in range(1, devices):
             peer = lax.rem(me + k, devices)
-            send(rs_send.at[turn, lax.rem(peer, groups)], rs_recv.at[turn, me], r_send.at[turn, peer], r_recv.at[turn, me], peer)
-        rs_recv[turn, me] = rs_send[turn, group]
-        for k in range(1, devices):
-            peer = lax.rem(me + k, devices)
-            arrive(rs_recv.at[turn, peer], r_recv.at[turn, peer])
-        ag_send[turn] = jnp.sum(rs_recv[turn], axis=0)
-        for k in range(1, groups):
-            g = lax.rem(group + k, groups)
-            send(ag_send.at[turn], ag_recv.at[turn, group], g_send.at[turn, g], g_recv.at[turn, group], slab * groups + g)
-        ag_recv[turn, group] = ag_send[turn]
-        for k in range(1, groups):
-            g = lax.rem(group + k, groups)
-            arrive(ag_recv.at[turn, g], g_recv.at[turn, g])
-        return ag_recv[turn].reshape(K, 128)
+            arrive(half_recv.at[turn, peer], h_recv.at[turn, peer])
+        return jnp.sum(half_recv[turn].reshape(devices // 2, K // 2, 128), axis=0)
 
     both_one = eliminate(summed(matrix, 0, highest))
     basis_one = jnp.dot(both_one[:, K:], matrix, precision=highest, preferred_element_type=jnp.float32)
@@ -187,8 +188,8 @@
         send(back_send.at[g], q_out.at[group], b_send.at[g], b_recv.at[group], slab * groups + g)
     q_out[group] = back_send[group]
     first = both_one[:, :K]
-    first_out[...] = first * (1.0 / scale)
-    r_out[...] = jnp.dot(both_two[:, :K], first, precision=highest, preferred_element_type=jnp.float32) * (1.0 / scale)
+    r = jnp.dot(both_two[:, :K], first, precision=highest, preferred_element_type=jnp.float32)
+    factors_out[...] = jnp.concatenate([r, first], axis=1) * (1.0 / scale)
     for k in range(1, groups):
         g = lax.rem(group + k, groups)
         arrive(q_out.at[g], b_recv.at[g])
@@ -209,37 +210,38 @@
     block = (groups, chunk, probe, depth)
     f32 = jnp.float32
     vmem = pl.BlockSpec(memory_space=pltpu.VMEM)
-    q, r, first = pl.pallas_call(
+    q, factors = pl.pallas_call(
         functools.partial(kernel, slabs, groups, scale),
         out_shape=(
             jax.ShapeDtypeStruct(block, f32),
-            jax.ShapeDtypeStruct((K, K), f32),
-            jax.ShapeDtypeStruct((K, K), f32),
+            jax.ShapeDtypeStruct((K, 2 * K), f32),
         ),
-        in_specs=[vmem],
-        out_specs=(vmem, vmem, vmem),
+        in_specs=[pl.BlockSpec(memory_space=pl.ANY)],
+        out_specs=(vmem, vmem),
         scratch_shapes=[
+            pltpu.VMEM((probe * cells, depth), f32),
             pltpu.VMEM(block, f32),
             pltpu.VMEM((others,) + block, f32),
             pltpu.VMEM(block, f32),
             pltpu.VMEM((others,) + block, f32),
-            pltpu.VMEM((2, groups, probe, 128), f32),
-            pltpu.VMEM((2, devices, probe, 128), f32),
-            pltpu.VMEM((2, probe, 128), f32),
-            pltpu.VMEM((2, groups, probe, 128), f32),
+            pltpu.VMEM((2, 2, K // 4, 128), f32),
+            pltpu.VMEM((2, K // 4, 128), f32),
+            pltpu.VMEM((2, K // 4, 128), f32),
+            pltpu.VMEM((2, devices, K // 4, 128), f32),
             pltpu.VMEM(block, f32),
             dma((groups,)), dma((groups,)),
             dma((others, groups)), dma((others, groups)),
+            dma((2,)), dma((2,)),
             dma((2, devices)), dma((2, devices)),
-            dma((2, groups)), dma((2, groups)),
             dma((groups,)), dma((groups,)),
+            dma(()),
         ],
         compiler_params=pltpu.CompilerParams(
-            collective_id=0, has_side_effects=True, vmem_limit_bytes=48 * 1024 * 1024
+            collective_id=0, has_side_effects=True, vmem_limit_bytes=60 * 1024 * 1024
         ),
     )(actions.reshape(probe * cells, depth))
     q_fields = q.reshape(cells, probe, depth).transpose(1, 0, 2)
-    return (q_fields.reshape(1, probe, width, rows_y, depth), r, first)
+    return (q_fields.reshape(1, probe, width, rows_y, depth), factors[:, :K], factors[:, K:])
 
 
 def solution(mesh):

time: 40.4 us -> 38.6 us (0.955)
  Pallas kernels: 36.8 us -> 35.5 us
  local copies, waits for them, and re-layouts: 2.81 us -> 2.29 us
    unnamed x4 -> x2, local copies, waits for them, and re-layouts: 2.13 us -> 0.01 us
    pallas_call x1, Pallas kernels: 36.8 us -> 35.5 us  [shards(): pl.pallas_call(functools.partial(kernel, slabs, groups, scale), out_shape...]
    transpose x1, local copies, waits for them, and re-layouts: 0.68 us -> 1.59 us  [shards(): q_fields = q.reshape(cells, probe, depth).transpose(1, 0, 2)]
    slice x0 -> x1, local copies, waits for them, and re-layouts: none -> 0.69 us  [shards(): factors[:, K:]]
where the time goes in v2:
time: 38.6 us; the launch traced here: 38.5 us
  Pallas kernels  35.5 us (92%)
  local copies, waits for them, and re-layouts  2.29 us (6%)
  between operations  0.65 us (2%)
    pallas_call x1, Pallas kernels, shards(): pl.pallas_call(functools.partial(kernel, slabs, groups, scale), out_shape...  35.5 us
    transpose x1, local copies, waits for them, and re-layouts, shards(): q_fields = q.reshape(cells, probe, depth).transpose(1, 0, 2)  1.59 us

profile of v2, /device:TPU:0, one launch (start us, length us, event | category | flops | bytes accessed | tf_op | source)
XLA Modules:
  0.0 38.5 jit_solution(10429239224695637749)
XLA Ops:
  0.6 35.5 %shard_map.38 = (f32[8,4,8,128]{3,2,1,0:T(8,128)}, f32[64,128]{1,0:T(8,128)}) custom-call(f32[256,128]{1,0:T(8,128)} %bitcast.5), custom_call_target="tpu_custom_call" | custom-call | tf_op jit(solution)/shard_map/pallas_call | solution.py:213
  36.2 0.0 copy-start
  36.2 1.6 %copy.4 = f32[8,32,128]{2,1,0:T(8,128)} copy(f32[8,32,128]{2,0,1:T(8,128)} %bitcast.7) | data formatting | bytes 262144 | tf_op jit(solution)/shard_map/transpose | solution.py:243
  37.8 0.0 copy-done
  37.8 0.7 %fusion = (f32[64,64]{1,0:T(8,128)}, f32[64,64]{1,0:T(8,128)}) fusion(f32[64,128]{1,0:T(8,128)S(1)} %copy-done), kind=kLoop, calls=%fused_computation | loop fusion | bytes 65536 | tf_op jit(solution)/shard_map/slice | solution.py:244
Async XLA Ops:
  36.2 1.6 %copy-start = (f32[64,128]{1,0:T(8,128)S(1)}, f32[64,128]{1,0:T(8,128)}, u32[]{:S(2)}) copy-start(f32[64,128]{1,0:T(8,128)} %get-tuple-element.6) | copy-start | bytes 98308

commit v3 on v2

--- a/solution.py
+++ b/solution.py
@@ -68,7 +68,7 @@
     slabs, groups, scale,
     source, q_out, factors_out,
     fields,
-    own_send, cross_send, own_recv, cross_recv, part_send, part_recv, half_send, half_recv, back_send,
+    own_send, cross_send, own_recv, cross_recv, part_send, part_recv, half_send, half_recv, mine, slab_rows, inverses,
     a_send, a_recv, c_send, c_recv, p_send, p_recv, h_send, h_recv, b_send, b_recv, in_sem,
 ):
     devices = slabs * groups
@@ -157,11 +157,29 @@
     total = own_recv[...]
     for n in range(len(offsets)):
         total = total + cross_recv[n]
-    matrix = jnp.concatenate([total[:, c].reshape(K, 128) for c in range(chunk)], axis=1)
-
-    def summed(rows, turn, precision):
+    for c in range(chunk):
+        mine[c] = total[:, c].reshape(K, 128)
+    matrix = jnp.concatenate([mine[c] for c in range(chunk)], axis=1)
+
+    beside_me = 1 - 2 * core
+
+    def share():
+        for k in reversed(range(2, groups, 2)):
+            g = lax.rem(group + k, groups)
+            send(mine, slab_rows.at[group], b_send.at[g], b_recv.at[group], slab * groups + g)
+        g = group + beside_me
+        send(mine, slab_rows.at[group], b_send.at[g], b_recv.at[group], slab * groups + g)
+        slab_rows[group] = mine[...]
+
+    def relay():
+        for k in range(2, groups, 2):
+            g = lax.rem(group + k, groups)
+            arrive(slab_rows.at[g], b_recv.at[g])
+            send(slab_rows.at[g], slab_rows.at[g], b_send.at[g + beside_me], b_recv.at[g], me + beside_me)
+
+    def summed(rows, turn, beside):
         part = lax.dot_general(
-            rows, rows, (((1,), (1,)), ((), ())), precision=precision, preferred_element_type=jnp.float32
+            rows, rows, (((1,), (1,)), ((), ())), precision=highest, preferred_element_type=jnp.float32
         )
         part = jnp.concatenate([part[: K // 2], part[K // 2 :]], axis=1)
         part_send[turn] = part.reshape(2, K // 4, 128)
@@ -172,27 +190,29 @@
             peer = lax.rem(me + k, devices)
             send(half_send.at[turn], half_recv.at[turn, me], h_send.at[turn, peer], h_recv.at[turn, me], peer)
         half_recv[turn, me] = half_send[turn]
+        beside()
         for k in range(1, devices):
             peer = lax.rem(me + k, devices)
             arrive(half_recv.at[turn, peer], h_recv.at[turn, peer])
         return jnp.sum(half_recv[turn].reshape(devices // 2, K // 2, 128), axis=0)
 
-    both_one = eliminate(summed(matrix, 0, highest))
+    both_one = eliminate(summed(matrix, 0, share))
     basis_one = jnp.dot(both_one[:, K:], matrix, precision=highest, preferred_element_type=jnp.float32)
-    both_two = eliminate(summed(basis_one, 1, highest))
-    basis = jnp.dot(both_two[:, K:] * scale, basis_one, precision=highest, preferred_element_type=jnp.float32)
-    for c in range(chunk):
-        back_send[:, c] = basis[:, 128 * c : 128 * c + 128].reshape(groups, probe, 128)
-    for k in range(1, groups):
-        g = lax.rem(group + k, groups)
-        send(back_send.at[g], q_out.at[group], b_send.at[g], b_recv.at[group], slab * groups + g)
-    q_out[group] = back_send[group]
+    both_two = eliminate(summed(basis_one, 1, relay))
+    product = jnp.dot(both_two[:, K:] * scale, both_one[:, K:], precision=highest, preferred_element_type=jnp.float32)
+    inverses[:, :K] = product
+    weights = inverses[pl.ds(pl.multiple_of(group * probe, probe), probe), :][:, :K]
+    for k in range(0, groups, 2):
+        g = lax.rem(group + k, groups) + beside_me
+        arrive(slab_rows.at[g], b_recv.at[g])
+    for g in range(groups):
+        rows = jnp.concatenate([slab_rows[g, c] for c in range(chunk)], axis=1)
+        basis = jnp.dot(weights, rows, precision=highest, preferred_element_type=jnp.float32)
+        for c in range(chunk):
+            q_out[g, c] = basis[:, 128 * c : 128 * c + 128]
     first = both_one[:, :K]
     r = jnp.dot(both_two[:, :K], first, precision=highest, preferred_element_type=jnp.float32)
     factors_out[...] = jnp.concatenate([r, first], axis=1) * (1.0 / scale)
-    for k in range(1, groups):
-        g = lax.rem(group + k, groups)
-        arrive(q_out.at[g], b_recv.at[g])
     for copy in started:
         copy.wait_send()
 
@@ -216,7 +236,7 @@
             jax.ShapeDtypeStruct(block, f32),
             jax.ShapeDtypeStruct((K, 2 * K), f32),
         ),
-        in_specs=[pl.BlockSpec(memory_space=pl.ANY)],
+        in_specs=[pl.BlockSpec(memory_space=pltpu.HBM)],
         out_specs=(vmem, vmem),
         scratch_shapes=[
             pltpu.VMEM((probe * cells, depth), f32),
@@ -228,7 +248,9 @@
             pltpu.VMEM((2, K // 4, 128), f32),
             pltpu.VMEM((2, K // 4, 128), f32),
             pltpu.VMEM((2, devices, K // 4, 128), f32),
-            pltpu.VMEM(block, f32),
+            pltpu.VMEM((chunk, K, depth), f32),
+            pltpu.VMEM((groups, chunk, K, depth), f32),
+            pltpu.VMEM((K, 128), f32),
             dma((groups,)), dma((groups,)),
             dma((others, groups)), dma((others, groups)),
             dma((2,)), dma((2,)),
@@ -237,7 +259,7 @@
             dma(()),
         ],
         compiler_params=pltpu.CompilerParams(
-            collective_id=0, has_side_effects=True, vmem_limit_bytes=60 * 1024 * 1024
+            collective_id=0, has_side_effects=True, vmem_limit_bytes=20 * 1024 * 1024 + 16 * 4 * math.prod(block)
         ),
     )(actions.reshape(probe * cells, depth))
     q_fields = q.reshape(cells, probe, depth).transpose(1, 0, 2)

time: 38.6 us -> 35.3 us (0.915)
  Pallas kernels: 35.5 us -> 32.3 us
    pallas_call x1, Pallas kernels: 35.5 us -> 32.3 us  [shards(): pl.pallas_call(functools.partial(kernel, slabs, groups, scale), out_shape...]
    transpose x1, local copies, waits for them, and re-layouts: 1.59 us -> 0.68 us  [shards(): q_fields = q.reshape(cells, probe, depth).transpose(1, 0, 2)]
    unnamed x2, local copies, waits for them, and re-layouts: 0.01 us -> 0.9 us
where the time goes in v3:
time: 35.3 us; the launch traced here: 35.2 us
  Pallas kernels  32.3 us (92%)
  local copies, waits for them, and re-layouts  2.27 us (6%)
  between operations  0.65 us (2%)
    pallas_call x1, Pallas kernels, shards(): pl.pallas_call(functools.partial(kernel, slabs, groups, scale), out_shape...  32.3 us
    unnamed x2, local copies, waits for them, and re-layouts  0.9 us

profile of v3, /device:TPU:0, one launch (start us, length us, event | category | flops | bytes accessed | tf_op | source)
XLA Modules:
  0.0 35.2 jit_solution(11037340239351250362)
XLA Ops:
  0.6 0.0 copy-start
  0.6 0.9 %copy-done = f32[1,8,16,2,128]{4,3,2,1,0:T(2,128)S(1)} copy-done((f32[1,8,16,2,128]{4,3,2,1,0:T(2,128)S(1)}, f32[1,8,16,2,128]{4,3,2,1,0:T(2,128)}, u32[]{:S(2)}) %copy-start) | copy-done | bytes 131096
  1.5 32.3 %shard_map.38 = (f32[8,4,8,128]{3,2,1,0:T(8,128)S(1)}, f32[64,128]{1,0:T(8,128)S(1)}) custom-call(f32[256,128]{1,0:T(8,128)S(1)} %bitcast.5), custom_call_target="tpu_custom_call" | custom-call | tf_op jit(solution)/shard_map/pallas_call | solution.py:233
  33.8 0.7 %copy.4 = f32[8,32,128]{2,1,0:T(8,128)} copy(f32[8,32,128]{2,0,1:T(8,128)S(1)} %bitcast.6) | data formatting | bytes 262144 | tf_op jit(solution)/shard_map/transpose | solution.py:265
  34.5 0.7 %fusion = (f32[64,64]{1,0:T(8,128)}, f32[64,64]{1,0:T(8,128)}) fusion(f32[64,128]{1,0:T(8,128)S(1)} %get-tuple-element.6), kind=kLoop, calls=%fused_computation | loop fusion | bytes 65536 | tf_op jit(solution)/shard_map/slice | solution.py:266
Async XLA Ops:
  0.6 0.9 %copy-start = (f32[1,8,16,2,128]{4,3,2,1,0:T(2,128)S(1)}, f32[1,8,16,2,128]{4,3,2,1,0:T(2,128)}, u32[]{:S(2)}) copy-start(f32[1,8,16,2,128]{4,3,2,1,0:T(2,128)} %param.1) | copy-start | bytes 393220

commit v4 on v3

--- a/solution.py
+++ b/solution.py
@@ -68,7 +68,7 @@
     slabs, groups, scale,
     source, q_out, factors_out,
     fields,
-    own_send, cross_send, own_recv, cross_recv, part_send, part_recv, half_send, half_recv, mine, slab_rows, inverses,
+    own_send, cross_send, own_recv, cross_recv, part_send, part_recv, half_send, half_recv, mine, slab_rows, inverses, pair_rows,
     a_send, a_recv, c_send, c_recv, p_send, p_recv, h_send, h_recv, b_send, b_recv, in_sem,
 ):
     devices = slabs * groups
@@ -84,7 +84,7 @@
     load = pltpu.make_async_copy(source, fields, in_sem)
     load.start()
     barrier = pltpu.get_barrier_semaphore()
-    for k in range(1, devices):
+    for k in reversed(range(1, devices)):
         pl.semaphore_signal(barrier, inc=1, device_id={"space": lax.rem(me + k, devices)}, device_id_type=MESH)
 
     load.wait()
@@ -134,6 +134,10 @@
         )
         copy.start()
         started.append(copy)
+
+    def drain(limit):
+        while len(started) > limit:
+            started.pop(0).wait_send()
 
     def arrive(dst, sem):
         pltpu.make_async_copy(dst, dst, sem).wait()
@@ -177,32 +181,49 @@
             arrive(slab_rows.at[g], b_recv.at[g])
             send(slab_rows.at[g], slab_rows.at[g], b_send.at[g + beside_me], b_recv.at[g], me + beside_me)
 
-    def summed(rows, turn, beside):
+    def summed(rows):
+        before = len(started)
         part = lax.dot_general(
             rows, rows, (((1,), (1,)), ((), ())), precision=highest, preferred_element_type=jnp.float32
         )
         part = jnp.concatenate([part[: K // 2], part[K // 2 :]], axis=1)
-        part_send[turn] = part.reshape(2, K // 4, 128)
-        send(part_send.at[turn, 1 - core], part_recv.at[turn], p_send.at[turn], p_recv.at[turn], me + 1 - 2 * core)
-        arrive(part_recv.at[turn], p_recv.at[turn])
-        half_send[turn] = part_send[turn, core] + part_recv[turn]
+        part_send[...] = part.reshape(2, K // 4, 128)
+        send(part_send.at[1 - core], part_recv, p_send, p_recv, me + beside_me)
+        arrive(part_recv, p_recv)
+        return added(part_send[core] + part_recv[...], 0, share, before)
+
+    def added(half, turn, beside, before):
+        half_send[turn] = half
         for k in reversed(range(1, devices)):
             peer = lax.rem(me + k, devices)
             send(half_send.at[turn], half_recv.at[turn, me], h_send.at[turn, peer], h_recv.at[turn, me], peer)
         half_recv[turn, me] = half_send[turn]
         beside()
+        drain(len(started) - before)
         for k in range(1, devices):
             peer = lax.rem(me + k, devices)
             arrive(half_recv.at[turn, peer], h_recv.at[turn, peer])
         return jnp.sum(half_recv[turn].reshape(devices // 2, K // 2, 128), axis=0)
 
-    both_one = eliminate(summed(matrix, 0, share))
-    basis_one = jnp.dot(both_one[:, K:], matrix, precision=highest, preferred_element_type=jnp.float32)
-    both_two = eliminate(summed(basis_one, 1, relay))
+    both_one = eliminate(summed(matrix))
+    beside = group + beside_me
+    arrive(slab_rows.at[beside], b_recv.at[beside])
+    pair = jnp.concatenate([matrix] + [slab_rows[beside, c] for c in range(chunk)], axis=1)
+    basis_one = jnp.dot(both_one[:, K:], pair, precision=highest, preferred_element_type=jnp.float32)
+    pair_rows[...] = basis_one
+    quarter = K // 4
+    low = pl.multiple_of(core * quarter, quarter)
+    mine_low, mine_high = pair_rows[pl.ds(low, quarter), :], pair_rows[pl.ds(low + K // 2, quarter), :]
+    part = lax.dot_general(
+        jnp.concatenate([mine_low, mine_high], axis=0), basis_one, (((1,), (1,)), ((), ())),
+        precision=highest, preferred_element_type=jnp.float32,
+    )
+    part = jnp.concatenate([part[:quarter], part[quarter:]], axis=1)
+    both_two = eliminate(added(part, 1, relay, len(started)))
     product = jnp.dot(both_two[:, K:] * scale, both_one[:, K:], precision=highest, preferred_element_type=jnp.float32)
     inverses[:, :K] = product
     weights = inverses[pl.ds(pl.multiple_of(group * probe, probe), probe), :][:, :K]
-    for k in range(0, groups, 2):
+    for k in range(2, groups, 2):
         g = lax.rem(group + k, groups) + beside_me
         arrive(slab_rows.at[g], b_recv.at[g])
     for g in range(groups):
@@ -213,8 +234,15 @@
     first = both_one[:, :K]
     r = jnp.dot(both_two[:, :K], first, precision=highest, preferred_element_type=jnp.float32)
     factors_out[...] = jnp.concatenate([r, first], axis=1) * (1.0 / scale)
-    for copy in started:
-        copy.wait_send()
+    drain(0)
+
+
+def finish(blocks, factors, q_out, r_out, first_out):
+    cells, probe, _ = blocks.shape
+    for c in range(cells):
+        q_out[pl.ds(c, probe, stride=cells), :] = blocks[c]
+    r_out[...] = factors[:, :K]
+    first_out[...] = factors[:, K:]
 
 
 def shards(actions):
@@ -244,16 +272,17 @@
             pltpu.VMEM((others,) + block, f32),
             pltpu.VMEM(block, f32),
             pltpu.VMEM((others,) + block, f32),
-            pltpu.VMEM((2, 2, K // 4, 128), f32),
             pltpu.VMEM((2, K // 4, 128), f32),
+            pltpu.VMEM((K // 4, 128), f32),
             pltpu.VMEM((2, K // 4, 128), f32),
             pltpu.VMEM((2, devices, K // 4, 128), f32),
             pltpu.VMEM((chunk, K, depth), f32),
             pltpu.VMEM((groups, chunk, K, depth), f32),
             pltpu.VMEM((K, 128), f32),
+            pltpu.VMEM((K, 2 * chunk * depth), f32),
             dma((groups,)), dma((groups,)),
             dma((others, groups)), dma((others, groups)),
-            dma((2,)), dma((2,)),
+            dma(()), dma(()),
             dma((2, devices)), dma((2, devices)),
             dma((groups,)), dma((groups,)),
             dma(()),
@@ -262,8 +291,18 @@
             collective_id=0, has_side_effects=True, vmem_limit_bytes=20 * 1024 * 1024 + 16 * 4 * math.prod(block)
         ),
     )(actions.reshape(probe * cells, depth))
-    q_fields = q.reshape(cells, probe, depth).transpose(1, 0, 2)
-    return (q_fields.reshape(1, probe, width, rows_y, depth), factors[:, :K], factors[:, K:])
+    q_fields, r, first = pl.pallas_call(
+        finish,
+        out_shape=(
+            jax.ShapeDtypeStruct((probe * cells, depth), f32),
+            jax.ShapeDtypeStruct((K, K), f32),
+            jax.ShapeDtypeStruct((K, K), f32),
+        ),
+        in_specs=[vmem, vmem],
+        out_specs=(vmem, vmem, vmem),
+        compiler_params=pltpu.CompilerParams(vmem_limit_bytes=16 * 1024 * 1024),
+    )(q.reshape(cells, probe, depth), factors)
+    return (q_fields.reshape(1, probe, width, rows_y, depth), r, first)
 
 
 def solution(mesh):

time: 35.3 us -> 34 us (0.963)
  local copies, waits for them, and re-layouts: 2.27 us -> 0.9 us
    pallas_call x0 -> x1, Pallas kernels: none -> 0.74 us  [shards(): pl.pallas_call(finish, out_shape=(jax.ShapeDtypeStruct((probe * cells, de...]
    pallas_call x1, Pallas kernels: 32.3 us -> 31.6 us  [shards(): pl.pallas_call(functools.partial(kernel, slabs, groups, scale), out_shape...]
    slice x1 -> x0, local copies, waits for them, and re-layouts: 0.69 us -> none  [shards(): factors[:, K:]]
    transpose x1 -> x0, local copies, waits for them, and re-layouts: 0.68 us -> none  [shards(): q_fields = q.reshape(cells, probe, depth).transpose(1, 0, 2)]
where the time goes in v4:
time: 34 us; the launch traced here: 33.9 us
  Pallas kernels  32.3 us (95%)
  local copies, waits for them, and re-layouts  0.9 us (3%)
  between operations  0.65 us (2%)
    pallas_call x1, Pallas kernels, shards(): pl.pallas_call(functools.partial(kernel, slabs, groups, scale), out_shape...  31.6 us
    unnamed x2, local copies, waits for them, and re-layouts  0.9 us
    pallas_call x1, Pallas kernels, shards(): pl.pallas_call(finish, out_shape=(jax.ShapeDtypeStruct((probe * cells, de...  0.74 us

profile of v4, /device:TPU:0, one launch (start us, length us, event | category | flops | bytes accessed | tf_op | source)
XLA Modules:
  0.0 33.9 jit_solution(17709211879739229391)
XLA Ops:
  0.6 0.0 copy-start
  0.6 0.9 %copy-done = f32[1,8,16,2,128]{4,3,2,1,0:T(2,128)S(1)} copy-done((f32[1,8,16,2,128]{4,3,2,1,0:T(2,128)S(1)}, f32[1,8,16,2,128]{4,3,2,1,0:T(2,128)}, u32[]{:S(2)}) %copy-start) | copy-done | bytes 131096
  1.5 31.6 %shard_map.38 = (f32[8,4,8,128]{3,2,1,0:T(8,128)S(1)}, f32[64,128]{1,0:T(8,128)S(1)}) custom-call(f32[256,128]{1,0:T(8,128)S(1)} %bitcast.4), custom_call_target="tpu_custom_call" | custom-call | tf_op jit(solution)/shard_map/pallas_call | solution.py:261
  33.1 0.7 %shard_map.39 = (f32[256,128]{1,0:T(8,128)}, f32[64,64]{1,0:T(8,128)}, f32[64,64]{1,0:T(8,128)}) custom-call(f32[32,8,128]{2,1,0:T(8,128)S(1)} %bitcast.3, f32[64,128]{1,0:T(8,128)S(1)} %get-tuple-element.9.factors), custom_call_target="tpu_custom_call" | custom-call | tf_op jit(solution)/shard_map/pallas_call | solution.py:294
Async XLA Ops:
  0.6 0.9 %copy-start = (f32[1,8,16,2,128]{4,3,2,1,0:T(2,128)S(1)}, f32[1,8,16,2,128]{4,3,2,1,0:T(2,128)}, u32[]{:S(2)}) copy-start(f32[1,8,16,2,128]{4,3,2,1,0:T(2,128)} %param.1) | copy-start | bytes 393220

commit v5 on v4

--- a/solution.py
+++ b/solution.py
@@ -290,7 +290,7 @@
         compiler_params=pltpu.CompilerParams(
             collective_id=0, has_side_effects=True, vmem_limit_bytes=20 * 1024 * 1024 + 16 * 4 * math.prod(block)
         ),
-    )(actions.reshape(probe * cells, depth))
+    )(pltpu.with_memory_space_constraint(actions.reshape(probe * cells, depth), pltpu.HBM))
     q_fields, r, first = pl.pallas_call(
         finish,
         out_shape=(

time: 34 us -> 33 us (0.971)
  local copies, waits for them, and re-layouts: 0.9 us -> 0 us
    unnamed x2 -> x0, local copies, waits for them, and re-layouts: 0.9 us -> none
where the time goes in v5:
time: 33 us; the launch traced here: 32.9 us
  Pallas kernels  32.2 us (98%)
  between operations  0.64 us (2%)
    pallas_call x1, Pallas kernels, shards(): pl.pallas_call(functools.partial(kernel, slabs, groups, scale), out_shape...  31.5 us
    pallas_call x1, Pallas kernels, shards(): pl.pallas_call(finish, out_shape=(jax.ShapeDtypeStruct((probe * cells, de...  0.74 us

profile of v5, /device:TPU:0, one launch (start us, length us, event | category | flops | bytes accessed | tf_op | source)
XLA Modules:
  0.0 32.9 jit_solution(1598345918797293707)
XLA Ops:
  0.6 31.5 %shard_map.38 = (f32[8,4,8,128]{3,2,1,0:T(8,128)S(1)}, f32[64,128]{1,0:T(8,128)S(1)}) custom-call(f32[256,128]{1,0:T(8,128)} %bitcast.4), custom_call_target="tpu_custom_call" | custom-call | tf_op jit(solution)/shard_map/pallas_call | solution.py:261
  32.1 0.7 %shard_map.39 = (f32[256,128]{1,0:T(8,128)}, f32[64,64]{1,0:T(8,128)}, f32[64,64]{1,0:T(8,128)}) custom-call(f32[32,8,128]{2,1,0:T(8,128)S(1)} %bitcast.3, f32[64,128]{1,0:T(8,128)S(1)} %get-tuple-element.9.factors), custom_call_target="tpu_custom_call" | custom-call | tf_op jit(solution)/shard_map/pallas_call | solution.py:294

commit v6 on v5

--- a/solution.py
+++ b/solution.py
@@ -123,6 +123,7 @@
     for n, offset in enumerate(offsets):
         cross_send[n] = spread(lax.rem(slab + offset, slabs), False)
 
+    own_send[...] = spread(slab, True)
     pl.semaphore_wait(barrier, devices - 1)
 
     started = []
@@ -147,7 +148,6 @@
         for k in range(groups):
             g = lax.rem(group + k, groups)
             send(cross_send.at[n, g], cross_recv.at[n, group], c_send.at[n, g], c_recv.at[n, group], there * groups + g)
-    own_send[...] = spread(slab, True)
     for k in range(1, groups):
         g = lax.rem(group + k, groups)
         send(own_send.at[g], own_recv.at[group], a_send.at[g], a_recv.at[group], slab * groups + g)

time: 33 us -> 33 us (level)
  no operation moved by 1% of the time
where the time goes in v6:
time: 33 us; the launch traced here: 32.9 us
  Pallas kernels  32.2 us (98%)
  between operations  0.64 us (2%)
    pallas_call x1, Pallas kernels, shards(): pl.pallas_call(functools.partial(kernel, slabs, groups, scale), out_shape...  31.5 us
    pallas_call x1, Pallas kernels, shards(): pl.pallas_call(finish, out_shape=(jax.ShapeDtypeStruct((probe * cells, de...  0.74 us

profile of v6, /device:TPU:0, one launch (start us, length us, event | category | flops | bytes accessed | tf_op | source)
XLA Modules:
  0.0 32.9 jit_solution(12954870690261086420)
XLA Ops:
  0.6 31.5 %shard_map.38 = (f32[8,4,8,128]{3,2,1,0:T(8,128)S(1)}, f32[64,128]{1,0:T(8,128)S(1)}) custom-call(f32[256,128]{1,0:T(8,128)} %bitcast.4), custom_call_target="tpu_custom_call" | custom-call | tf_op jit(solution)/shard_map/pallas_call | solution.py:261
  32.1 0.7 %shard_map.39 = (f32[256,128]{1,0:T(8,128)}, f32[64,64]{1,0:T(8,128)}, f32[64,64]{1,0:T(8,128)}) custom-call(f32[32,8,128]{2,1,0:T(8,128)S(1)} %bitcast.3, f32[64,128]{1,0:T(8,128)S(1)} %get-tuple-element.9.factors), custom_call_target="tpu_custom_call" | custom-call | tf_op jit(solution)/shard_map/pallas_call | solution.py:294
